TPU v7x, 128 devices: a whole 4x4x4 slice. The times are simulated.
128 devices in a mesh: rep: 2 (over y_lo), fsdp: 8 (over z, y_hi), tp: 8 (over x, core).
Axes of the slice: x: 4, y: 4 (y_hi: 2, y_lo: 2; y = y_hi * 2 + y_lo), z: 4, core: 2. Of those that a mesh axis runs over, the one named last changes fastest.
Arguments:
- images: bfloat16 [16, 577, 1024], P(('rep', 'fsdp')), may hold values from -6 to 6
- cotangent: bfloat16 [16, 577, 1024], P(('rep', 'fsdp')), may hold values from -6 to 6
- norm1_gain: float32 [2, 1024], replicated, may hold values from 0.1 to 1.9
- norm1_shift: float32 [2, 1024], replicated, may hold values from -3 to 3
- qkv_weight: bfloat16 [2, 1024, 3, 1024], P(None, 'fsdp', None, 'tp'), may hold values from -0.1875 to 0.1875
- qv_bias: float32 [2, 2, 1024], P(None, None, 'tp'), may hold values from -3 to 3
- out_weight: bfloat16 [2, 1024, 1024], P(None, 'tp', 'fsdp'), may hold values from -0.75 to 0.75
- out_bias: float32 [2, 1024], replicated, may hold values from -3 to 3
- norm2_gain: float32 [2, 1024], replicated, may hold values from 0.1 to 1.9
- norm2_shift: float32 [2, 1024], replicated, may hold values from -3 to 3
- up_weight: bfloat16 [2, 1024, 4096], P(None, 'fsdp', 'tp'), may hold values from -0.1875 to 0.1875
- up_bias: float32 [2, 4096], P(None, 'tp'), may hold values from -3 to 3
- down_weight: bfloat16 [2, 4096, 1024], P(None, 'tp', 'fsdp'), may hold values from -0.09375 to 0.09375
- down_bias: float32 [2, 1024], replicated, may hold values from -5 to 5
Outputs:
- out_act: float32 [16, 577, 1024], P(('rep', 'fsdp'))
- grad_images: float32 [16, 577, 1024], P(('rep', 'fsdp'))
- grad_norm1_gain: float32 [2, 1024], replicated
- grad_norm1_shift: float32 [2, 1024], replicated
- grad_qkv_weight: float32 [2, 1024, 3, 1024], P(None, 'fsdp', None, 'tp')
- grad_qv_bias: float32 [2, 2, 1024], P(None, None, 'tp')
- grad_out_weight: float32 [2, 1024, 1024], P(None, 'tp', 'fsdp')
- grad_out_bias: float32 [2, 1024], replicated
- grad_norm2_gain: float32 [2, 1024], replicated
- grad_norm2_shift: float32 [2, 1024], replicated
- grad_up_weight: float32 [2, 1024, 4096], P(None, 'fsdp', 'tp')
- grad_up_bias: float32 [2, 4096], P(None, 'tp')
- grad_down_weight: float32 [2, 4096, 1024], P(None, 'tp', 'fsdp')
- grad_down_bias: float32 [2, 1024], replicated
All inputs are finite; a program needn't handle non-finite values.
Results may differ from a plain program's by a relative error of at most 0.012.
Values may be sent and summed in bfloat16 or wider, within the bound.
No kernel may reach another device: no remote copies, remote signals or barrier semaphores. Data moves between devices by JAX's collectives and lax.ppermute only.
A program may use at most 128 MiB of HBM per device.

v0:
```python
import jax
import jax.numpy as jnp
from jax import lax
from jax.sharding import PartitionSpec as P

HEAD_DIM = 64
EPSILON = 1e-05


def norm_forward(values_in, norm_gain, norm_shift):
    row_mean = jnp.mean(values_in, -1, keepdims=True)
    centred = values_in - row_mean
    inv_std = lax.rsqrt(jnp.mean(centred * centred, -1, keepdims=True) + EPSILON)
    normed = centred * inv_std
    return (normed * norm_gain + norm_shift, normed, inv_std)


def norm_backward(upstream, normed, inv_std, norm_gain):
    scaled = upstream * norm_gain
    return inv_std * (
        scaled
        - jnp.mean(scaled, -1, keepdims=True)
        - normed * jnp.mean(scaled * normed, -1, keepdims=True)
    )


def gelu_parts(pre_act):
    normal_cdf = 0.5 * (1.0 + lax.erf(pre_act * 0.7071067811865476))
    normal_pdf = jnp.exp(-0.5 * pre_act * pre_act) * 0.3989422804014327
    return (pre_act * normal_cdf, normal_cdf + pre_act * normal_pdf)


def attend(queries, key_vecs, val_vecs):
    softmax_scale = HEAD_DIM ** (-0.5)
    scores = (
        jnp.einsum("bqhe,bkhe->bhqk", queries, key_vecs, preferred_element_type=jnp.float32)
        * softmax_scale
    )
    row_max = jnp.max(scores, -1, keepdims=True)
    log_total = row_max + jnp.log(jnp.sum(jnp.exp(scores - row_max), -1, keepdims=True))
    prob_b = jnp.exp(scores - log_total).astype(jnp.bfloat16)
    mixed_b = jnp.einsum(
        "bhqk,bkhe->bqhe", prob_b, val_vecs, preferred_element_type=jnp.float32
    ).astype(jnp.bfloat16)
    return (mixed_b, log_total)


def attend_back(queries, key_vecs, val_vecs, log_total, d_mixed):
    softmax_scale = HEAD_DIM ** (-0.5)
    scores = (
        jnp.einsum("bqhe,bkhe->bhqk", queries, key_vecs, preferred_element_type=jnp.float32)
        * softmax_scale
    )
    probs = jnp.exp(scores - log_total)
    prob_b = probs.astype(jnp.bfloat16)
    d_values = jnp.einsum("bhqk,bqhe->bkhe", prob_b, d_mixed, preferred_element_type=jnp.float32)
    d_probs = jnp.einsum("bqhe,bkhe->bhqk", d_mixed, val_vecs, preferred_element_type=jnp.float32)
    row_dot = jnp.sum(probs * d_probs, -1, keepdims=True)
    d_scores = (probs * (d_probs - row_dot) * softmax_scale).astype(jnp.bfloat16)
    d_queries = jnp.einsum(
        "bhqk,bkhe->bqhe", d_scores, key_vecs, preferred_element_type=jnp.float32
    )
    d_keys = jnp.einsum("bhqk,bqhe->bkhe", d_scores, queries, preferred_element_type=jnp.float32)
    return (d_queries, d_keys, d_values)


def branch_total(contrib):
    return lax.psum(contrib, "tp")


def input_total(contrib):
    return lax.psum(contrib, "tp")


def body(
    images,
    cotangent,
    norm1_gain,
    norm1_shift,
    qkv_weight,
    qv_bias,
    out_weight,
    out_bias,
    norm2_gain,
    norm2_shift,
    up_weight,
    up_bias,
    down_weight,
    down_bias,
):
    images_here, seq_len, model_width = images.shape
    row_count = images_here * seq_len
    layer_count = qkv_weight.shape[0]
    local_cols = qkv_weight.shape[3]
    heads_here = local_cols // HEAD_DIM
    head_shape = (images_here, seq_len, heads_here, HEAD_DIM)
    state = images.astype(jnp.float32).reshape(row_count, model_width)
    gradient = cotangent.astype(jnp.float32).reshape(row_count, model_width)
    saved = []
    for layer_idx in range(layer_count):
        qkv_full, out_full, up_full, down_full = (
            lax.all_gather(qkv_weight[layer_idx], "fsdp", axis=0, tiled=True),
            lax.all_gather(out_weight[layer_idx], "fsdp", axis=1, tiled=True),
            lax.all_gather(up_weight[layer_idx], "fsdp", axis=0, tiled=True),
            lax.all_gather(down_weight[layer_idx], "fsdp", axis=1, tiled=True),
        )
        normed_a, unit_a, inv_a = norm_forward(state, norm1_gain[layer_idx], norm1_shift[layer_idx])
        first_b = normed_a.astype(jnp.bfloat16)
        projected = jnp.einsum("rd,dtc->rtc", first_b, qkv_full, preferred_element_type=jnp.float32)
        queries = (projected[:, 0] + qv_bias[layer_idx, 0]).astype(jnp.bfloat16).reshape(head_shape)
        key_vecs = projected[:, 1].astype(jnp.bfloat16).reshape(head_shape)
        val_vecs = (
            (projected[:, 2] + qv_bias[layer_idx, 1]).astype(jnp.bfloat16).reshape(head_shape)
        )
        mixed_b, log_total = attend(queries, key_vecs, val_vecs)
        mixed_flat = mixed_b.reshape(row_count, local_cols)
        middle = (
            state
            + branch_total(jnp.dot(mixed_flat, out_full, preferred_element_type=jnp.float32))
            + out_bias[layer_idx]
        )
        normed_b, unit_b, inv_b = norm_forward(
            middle, norm2_gain[layer_idx], norm2_shift[layer_idx]
        )
        second_b = normed_b.astype(jnp.bfloat16)
        hidden = jnp.dot(second_b, up_full, preferred_element_type=jnp.float32) + up_bias[layer_idx]
        active, slopes = gelu_parts(hidden)
        active_b = active.astype(jnp.bfloat16)
        state = (
            middle
            + branch_total(jnp.dot(active_b, down_full, preferred_element_type=jnp.float32))
            + down_bias[layer_idx]
        )
        stored = ()
        saved.append(
            (
                stored,
                unit_a,
                inv_a,
                first_b,
                queries,
                key_vecs,
                val_vecs,
                log_total,
                mixed_flat,
                unit_b,
                inv_b,
                second_b,
                slopes,
                active_b,
            )
        )
    owned_grads = [None] * layer_count
    small_grads = [None] * layer_count
    for layer_idx in reversed(range(layer_count)):
        (
            stored,
            unit_a,
            inv_a,
            first_b,
            queries,
            key_vecs,
            val_vecs,
            log_total,
            mixed_flat,
            unit_b,
            inv_b,
            second_b,
            slopes,
            active_b,
        ) = saved[layer_idx]
        qkv_full, out_full, up_full, down_full = (
            lax.all_gather(qkv_weight[layer_idx], "fsdp", axis=0, tiled=True),
            lax.all_gather(out_weight[layer_idx], "fsdp", axis=1, tiled=True),
            lax.all_gather(up_weight[layer_idx], "fsdp", axis=0, tiled=True),
            lax.all_gather(down_weight[layer_idx], "fsdp", axis=1, tiled=True),
        )
        d_down_bias = jnp.sum(gradient, 0)
        grad_b = gradient.astype(jnp.bfloat16)
        d_down = jnp.einsum("rf,rd->fd", active_b, grad_b, preferred_element_type=jnp.float32)
        d_hidden = (
            jnp.einsum("rd,fd->rf", grad_b, down_full, preferred_element_type=jnp.float32) * slopes
        )
        d_up_bias = jnp.sum(d_hidden, 0)
        d_hidden_b = d_hidden.astype(jnp.bfloat16)
        d_up = jnp.einsum("rd,rf->df", second_b, d_hidden_b, preferred_element_type=jnp.float32)
        d_norm_two = input_total(
            jnp.einsum("rf,df->rd", d_hidden_b, up_full, preferred_element_type=jnp.float32)
        )
        d_gain_two = jnp.sum(d_norm_two * unit_b, 0)
        d_shift_two = jnp.sum(d_norm_two, 0)
        grad_mid = gradient + norm_backward(d_norm_two, unit_b, inv_b, norm2_gain[layer_idx])
        d_out_bias = jnp.sum(grad_mid, 0)
        mid_b = grad_mid.astype(jnp.bfloat16)
        d_out = jnp.einsum("rc,rd->cd", mixed_flat, mid_b, preferred_element_type=jnp.float32)
        d_mixed = (
            jnp.einsum("rd,cd->rc", mid_b, out_full, preferred_element_type=jnp.float32)
            .astype(jnp.bfloat16)
            .reshape(head_shape)
        )
        d_queries, d_keys, d_values = attend_back(queries, key_vecs, val_vecs, log_total, d_mixed)
        d_queries = d_queries.reshape(row_count, local_cols)
        d_keys = d_keys.reshape(row_count, local_cols)
        d_values = d_values.reshape(row_count, local_cols)
        d_qv_bias = jnp.stack([jnp.sum(d_queries, 0), jnp.sum(d_values, 0)])
        d_proj_b = jnp.stack([d_queries, d_keys, d_values], 1).astype(jnp.bfloat16)
        d_qkv = jnp.einsum("rd,rtc->dtc", first_b, d_proj_b, preferred_element_type=jnp.float32)
        d_norm_one = input_total(
            jnp.einsum("rtc,dtc->rd", d_proj_b, qkv_full, preferred_element_type=jnp.float32)
        )
        d_gain_one = jnp.sum(d_norm_one * unit_a, 0)
        d_shift_one = jnp.sum(d_norm_one, 0)
        gradient = grad_mid + norm_backward(d_norm_one, unit_a, inv_a, norm1_gain[layer_idx])
        small_grads[layer_idx] = (
            d_gain_one,
            d_shift_one,
            d_qv_bias,
            d_out_bias,
            d_gain_two,
            d_shift_two,
            d_up_bias,
            d_down_bias,
        )
        shares = (
            lax.psum_scatter(d_qkv, "fsdp", scatter_dimension=0, tiled=True),
            lax.psum_scatter(d_out, "fsdp", scatter_dimension=1, tiled=True),
            lax.psum_scatter(d_up, "fsdp", scatter_dimension=0, tiled=True),
            lax.psum_scatter(d_down, "fsdp", scatter_dimension=1, tiled=True),
        )
        owned_grads[layer_idx] = lax.psum((shares[0], shares[1], shares[2], shares[3]), "rep")
    big_grads = tuple(
        (
            jnp.stack([owned_grads[layer_idx][member] for layer_idx in range(layer_count)])
            for member in range(4)
        )
    )
    small_stack = [
        jnp.stack([small_grads[layer_idx][member] for layer_idx in range(layer_count)])
        for member in range(8)
    ]
    reduced = lax.psum(
        (
            small_stack[0],
            small_stack[1],
            small_stack[2],
            small_stack[3],
            small_stack[4],
            small_stack[5],
            small_stack[6],
            small_stack[7],
        ),
        ("rep", "fsdp"),
    )
    output = state.reshape(images_here, seq_len, model_width)
    grad_images = gradient.reshape(images_here, seq_len, model_width)
    return (
        output,
        grad_images,
        reduced[0],
        reduced[1],
        big_grads[0],
        reduced[2],
        big_grads[1],
        reduced[3],
        reduced[4],
        reduced[5],
        big_grads[2],
        reduced[6],
        big_grads[3],
        reduced[7],
    )


def solution(mesh):
    in_specs = (
        P(("rep", "fsdp"), None, None),
        P(("rep", "fsdp"), None, None),
        P(),
        P(),
        P(None, "fsdp", None, "tp"),
        P(None, None, "tp"),
        P(None, "tp", "fsdp"),
        P(),
        P(),
        P(),
        P(None, "fsdp", "tp"),
        P(None, "tp"),
        P(None, "tp", "fsdp"),
        P(),
    )
    out_specs = (
        P(("rep", "fsdp"), None, None),
        P(("rep", "fsdp"), None, None),
        P(),
        P(),
        P(None, "fsdp", None, "tp"),
        P(None, None, "tp"),
        P(None, "tp", "fsdp"),
        P(),
        P(),
        P(),
        P(None, "fsdp", "tp"),
        P(None, "tp"),
        P(None, "tp", "fsdp"),
        P(),
    )
    return jax.shard_map(body, mesh=mesh, in_specs=in_specs, out_specs=out_specs, check_vma=False)
```

profile of v0, /device:TPU:0, one launch (start us, length us, event | category | flops | bytes accessed | tf_op | source)
XLA Modules:
  0.0 1286.5 jit_solution(16832507435293279262)
XLA Ops:
  12.7 38.1 %all-gather = bf16[1,1024,3,128]{3,1,2,0:T(8,128)(2,1)S(1)} all-gather(bf16[1,128,3,128]{3,1,2,0:T(8,128)(2,1)S(1)} %get-tuple-element.109), channel_id=2, replica_groups=mesh['rep'=2,'fsdp'=8,'tp'=8] {'fsdp'}, dimensions={1}, use_global_device_ids=true | all-gather | bytes 884736 | tf_op jit(solution)/shard_map/all_gather | solution.py:102
  57.1 31.6 %all-gather.1 = bf16[1,128,1024]{2,1,0:T(8,128)(2,1)S(1)} all-gather(bf16[1,128,128]{2,1,0:T(8,128)(2,1)S(1)} %get-tuple-element.111), channel_id=3, replica_groups=mesh['rep'=2,'fsdp'=8,'tp'=8] {'fsdp'}, dimensions={2}, use_global_device_ids=true | all-gather | bytes 294912 | tf_op jit(solution)/shard_map/all_gather | solution.py:103
  97.5 63.3 %all-reduce.12.cloned.1.call-done = f32[577,1024]{1,0:T(8,128)} async-done(((f32[577,1024]{1,0:T(8,128)}), f32[577,1024]{1,0:T(8,128)}) %all-reduce.12.cloned.1.call-update) | async-done | bytes 2363408 | tf_op jit(solution)/shard_map/psum | solution.py:68
  164.5 3.3 convolution_add_fusion.1
  167.8 23.0 %all-gather.15.cloned.1.call-done = bf16[1,512,1024]{2,1,0:T(8,128)(2,1)} async-done(((bf16[1,512,128]{2,1,0:T(8,128)(2,1)}), bf16[1,512,1024]{2,1,0:T(8,128)(2,1)}) %all-gather.15.cloned.1.call-update) | async-done | bytes 1048592 | tf_op jit(solution)/shard_map/all_gather | solution.py:105
  190.7 3.8 fusion.78
  197.2 32.9 %all-gather.5 = bf16[1,128,1024]{2,1,0:T(8,128)(2,1)} all-gather(bf16[1,128,128]{2,1,0:T(8,128)(2,1)S(1)} %get-tuple-element.110), channel_id=7, replica_groups=mesh['rep'=2,'fsdp'=8,'tp'=8] {'fsdp'}, dimensions={2}, use_global_device_ids=true | all-gather | bytes 294912 | tf_op jit(solution)/shard_map/all_gather | solution.py:103
  231.5 40.0 %all-gather.4 = bf16[1,1024,3,128]{3,1,2,0:T(8,128)(2,1)} all-gather(bf16[1,128,3,128]{3,1,2,0:T(8,128)(2,1)} %get-tuple-element.108), channel_id=6, replica_groups=mesh['rep'=2,'fsdp'=8,'tp'=8] {'fsdp'}, dimensions={1}, use_global_device_ids=true | all-gather | bytes 884736 | tf_op jit(solution)/shard_map/all_gather | solution.py:102
  286.0 62.3 %all-reduce.16.cloned.1.call-done = f32[577,1024]{1,0:T(8,128)} async-done(((f32[577,1024]{1,0:T(8,128)}), f32[577,1024]{1,0:T(8,128)}) %all-reduce.16.cloned.1.call-update) | async-done | bytes 2363408 | tf_op jit(solution)/shard_map/psum | solution.py:68
  351.7 3.3 convolution_add_fusion
  355.1 23.3 %all-gather.19.cloned.1.call-done = bf16[1,512,1024]{2,1,0:T(8,128)(2,1)} async-done(((bf16[1,512,128]{2,1,0:T(8,128)(2,1)}), bf16[1,512,1024]{2,1,0:T(8,128)(2,1)}) %all-gather.19.cloned.1.call-update) | async-done | bytes 1048592 | tf_op jit(solution)/shard_map/all_gather | solution.py:105
  378.3 3.7 fusion.173
  385.4 64.8 %all-reduce.18.cloned.1.call-done = f32[577,1024]{1,0:T(8,128)} async-done(((f32[577,1024]{1,0:T(8,128)}), f32[577,1024]{1,0:T(8,128)}) %all-reduce.18.cloned.1.call-update) | async-done | bytes 2363408 | tf_op jit(solution)/shard_map/psum | solution.py:72
  450.2 3.4 multiply_reduce_fusion.4
  459.5 3.4 fusion.118
  462.9 7.3 fusion.156
  470.2 6.8 fusion.68
  477.1 3.8 fusion.157
  485.9 3.6 convolution_bitcast_fusion.1
  489.6 66.3 %all-reduce.20.cloned.1.call-done = f32[577,1024]{1,0:T(8,128)} async-done(((f32[577,1024]{1,0:T(8,128)}), f32[577,1024]{1,0:T(8,128)}) %all-reduce.20.cloned.1.call-update) | async-done | bytes 2363408 | tf_op jit(solution)/shard_map/psum | solution.py:72
  555.9 4.1 multiply_reduce_fusion.6
  560.1 3.3 fusion.144
  568.3 3.0 fusion.95
  571.5 3.7 fusion.101
  575.4 4.1 fusion.56
  579.5 4.3 fusion.115
  583.9 51.4 %all-reduce.22.cloned.1.call-done = f32[577,1024]{1,0:T(8,128)} async-done(((f32[577,1024]{1,0:T(8,128)}), f32[577,1024]{1,0:T(8,128)}) %all-reduce.22.cloned.1.call-update) | async-done | bytes 2363408 | tf_op jit(solution)/shard_map/psum | solution.py:72
  635.3 4.1 multiply_reduce_fusion.5
  639.4 3.2 fusion.145
  645.3 4.5 fusion.98
  649.9 4.4 fusion.92
  659.2 3.3 fusion.116
  662.5 6.8 fusion.154
  670.0 6.3 fusion.65
  677.1 3.2 fusion.155
  680.5 3.9 fusion.114
  684.5 3.9 fusion.72
  693.3 29.4 %reduce-scatter.19.cloned.1.call-done = f32[128,512]{1,0:T(8,128)} async-done(((f32[1024,512]{1,0:T(8,128)}), f32[128,512]{1,0:T(8,128)}) %reduce-scatter.19.cloned.1.call-update) | async-done | bytes 262160 | tf_op jit(solution)/shard_map/reduce_scatter | solution.py:227
  722.7 78.4 %reduce-scatter.23.cloned.1.call-done = f32[512,128]{1,0:T(8,128)} async-done(((f32[512,1024]{1,0:T(8,128)}), f32[512,128]{1,0:T(8,128)}) %reduce-scatter.23.cloned.1.call-update) | async-done | bytes 262160 | tf_op jit(solution)/shard_map/reduce_scatter | solution.py:228
  801.0 76.5 %reduce-scatter.11.cloned.1.call-done = f32[128,3,128]{2,0,1:T(8,128)} async-done(((f32[1024,3,128]{2,0,1:T(8,128)}), f32[128,3,128]{2,0,1:T(8,128)}) %reduce-scatter.11.cloned.1.call-update) | async-done | bytes 196624 | tf_op jit(solution)/shard_map/reduce_scatter | solution.py:225
  877.5 73.4 %reduce-scatter.13.cloned.1.call-done = f32[128,128]{1,0:T(8,128)} async-done(((f32[128,1024]{1,0:T(8,128)}), f32[128,128]{1,0:T(8,128)}) %reduce-scatter.13.cloned.1.call-update) | async-done | bytes 65552 | tf_op jit(solution)/shard_map/reduce_scatter | solution.py:226
  950.9 79.1 %reduce-scatter.17.cloned.1.call-done = f32[128,512]{1,0:T(8,128)} async-done(((f32[1024,512]{1,0:T(8,128)}), f32[128,512]{1,0:T(8,128)}) %reduce-scatter.17.cloned.1.call-update) | async-done | bytes 262160 | tf_op jit(solution)/shard_map/reduce_scatter | solution.py:227
  1030.1 78.3 %reduce-scatter.21.cloned.1.call-done = f32[512,128]{1,0:T(8,128)} async-done(((f32[512,1024]{1,0:T(8,128)}), f32[512,128]{1,0:T(8,128)}) %reduce-scatter.21.cloned.1.call-update) | async-done | bytes 262160 | tf_op jit(solution)/shard_map/reduce_scatter | solution.py:228
  1108.4 76.7 %reduce-scatter.9.cloned.1.call-done = f32[128,3,128]{2,0,1:T(8,128)} async-done(((f32[1024,3,128]{2,0,1:T(8,128)}), f32[128,3,128]{2,0,1:T(8,128)}) %reduce-scatter.9.cloned.1.call-update) | async-done | bytes 196624 | tf_op jit(solution)/shard_map/reduce_scatter | solution.py:225
  1185.1 3.2 fusion.25
  1190.8 3.8 copy.79
  1195.3 3.8 copy.78
  1199.2 73.4 %all-reduce = (f32[2,1024]{1,0:T(2,128)}, f32[2,1024]{1,0:T(2,128)}, f32[2,2,128]{2,1,0:T(2,128)}, f32[2,1024]{1,0:T(2,128)}, f32[2,1024]{1,0:T(2,128)}, /*index...) all-reduce(f32[2,1024]{1,0:T(2,128)S(1)} %pad_maximum_fusion.10, ...), channel_id=1, replica_groups=mesh['rep'=2,'fsdp'=8,'tp'=8] {'rep','fsdp'}, use_global_device_ids=true, to_apply=%region_32.0 | all-reduce | flops 13824 | bytes 110592 | tf_op jit(solution)/shard_map/psum | solution.py:241
  (322 shorter events, 87.8 us)
Async XLA Ops:
  8.0 43.4 %copy-start.10 = (bf16[1,577,1024]{2,1,0:T(8,128)(2,1)S(1)}, bf16[1,577,1024]{2,1,0:T(8,128)(2,1)}, u32[]{:S(2)}) copy-start(bf16[1,577,1024]{2,1,0:T(8,128)(2,1)} %param.14) | copy-start | bytes 3545092
  8.0 4.1 copy-start.42
  8.0 42.8 %copy-start.65 = (f32[2,1024]{1,0:T(2,128)S(1)}, f32[2,1024]{1,0:T(2,128)}, u32[]{:S(2)}) copy-start(f32[2,1024]{1,0:T(2,128)} %param.17) | copy-start | bytes 24580
  8.1 152.7 %all-reduce.12.cloned.1.call-start = ((), (), s32[]{:S(2)}) async-start(), calls=%async_computation.8 | async-start | bytes 4784128 | tf_op jit(solution)/shard_map/psum | solution.py:68
  11.5 41.1 %copy-start.47 = (f32[577]{0:T(1024)}, f32[577]{0:T(1024)S(1)}, u32[]{:S(2)}) copy-start(f32[577]{0:T(1024)S(1)} %add_rsqrt_fusion.3) | copy-start | bytes 6928
  12.1 40.5 %copy-start.50 = (f32[1,1024]{1,0:T(1,128)}, f32[1,1024]{1,0:T(1,128)S(1)}, u32[]{:S(2)}) copy-start(f32[1,1024]{1,0:T(1,128)S(1)} %get-tuple-element.119) | copy-start | bytes 12292
  57.1 36.2 %copy-start.69 = (f32[2,64]{1,0:T(2,128)}, f32[2,64]{1,0:T(2,128)S(1)}, u32[]{:S(2)}) copy-start(f32[2,64]{1,0:T(2,128)S(1)} %add.304) | copy-start | bytes 1540
  88.7 4.6 copy-start.20
  93.4 71.1 %all-gather.13.cloned.1.call-start = ((), (), s32[]{:S(2)}) async-start(), calls=%async_computation.22 | async-start | bytes 1179648 | tf_op jit(solution)/shard_map/all_gather | solution.py:104
  94.2 96.5 %all-gather.15.cloned.1.call-start = ((), (), s32[]{:S(2)}) async-start(), calls=%async_computation.23 | async-start | bytes 1179648 | tf_op jit(solution)/shard_map/all_gather | solution.py:105
  95.0 176.4 %all-reduce.14.cloned.1.call-start = ((), (), s32[]{:S(2)}) async-start(), calls=%async_computation.9 | async-start | bytes 4784128 | tf_op jit(solution)/shard_map/psum | solution.py:68
  163.2 108.3 %copy-start = (f32[577,1024]{1,0:T(8,128)}, f32[577,1024]{1,0:T(8,128)S(1)}, u32[]{:S(2)}) copy-start(f32[577,1024]{1,0:T(8,128)S(1)} %get-tuple-element.91) | copy-start | bytes 7090180
  194.6 153.7 %all-reduce.16.cloned.1.call-start = ((), (), s32[]{:S(2)}) async-start(), calls=%async_computation.10 | async-start | bytes 4784128 | tf_op jit(solution)/shard_map/psum | solution.py:68
  280.0 4.6 copy-start.18
  282.7 65.6 %copy-start.58 = (f32[1,1024]{1,0:T(1,128)S(1)}, f32[1,1024]{1,0:T(1,128)}, u32[]{:S(2)}) copy-start(f32[1,1024]{1,0:T(1,128)} %get-tuple-element.123) | copy-start | bytes 12292
  284.6 66.8 %all-gather.17.cloned.1.call-start = ((), (), s32[]{:S(2)}) async-start(), calls=%async_computation.24 | async-start | bytes 1179648 | tf_op jit(solution)/shard_map/all_gather | solution.py:104
  285.2 93.1 %all-gather.19.cloned.1.call-start = ((), (), s32[]{:S(2)}) async-start(), calls=%async_computation.25 | async-start | bytes 1179648 | tf_op jit(solution)/shard_map/all_gather | solution.py:105
  286.0 164.3 %all-reduce.18.cloned.1.call-start = ((), (), s32[]{:S(2)}) async-start(), calls=%async_computation.11 | async-start | bytes 4784128 | tf_op jit(solution)/shard_map/psum | solution.py:72
  378.3 4.6 copy-start.31
  385.2 170.7 %all-reduce.20.cloned.1.call-start = ((), (), s32[]{:S(2)}) async-start(), calls=%async_computation.12 | async-start | bytes 4784128 | tf_op jit(solution)/shard_map/psum | solution.py:72
  489.6 145.7 %all-reduce.22.cloned.1.call-start = ((), (), s32[]{:S(2)}) async-start(), calls=%async_computation.13 | async-start | bytes 4784128 | tf_op jit(solution)/shard_map/psum | solution.py:72
  555.9 4.1 copy-start.3
  555.9 4.1 copy-start.7
  568.2 125.0 %reduce-scatter.15.cloned.1.call-start = ((), (), s32[]{:S(2)}) async-start(), calls=%async_computation.17 | async-start | bytes 589824 | tf_op jit(solution)/shard_map/reduce_scatter | solution.py:226
  571.3 151.4 %reduce-scatter.19.cloned.1.call-start = ((), (), s32[]{:S(2)}) async-start(), calls=%async_computation.19 | async-start | bytes 2359296 | tf_op jit(solution)/shard_map/reduce_scatter | solution.py:227
  575.3 4.2 copy-start.76
  575.3 225.7 %reduce-scatter.23.cloned.1.call-start = ((), (), s32[]{:S(2)}) async-start(), calls=%async_computation.21 | async-start | bytes 2359296 | tf_op jit(solution)/shard_map/reduce_scatter | solution.py:228
  579.5 55.8 %copy-start.49 = (f32[577]{0:T(1024)S(1)}, f32[577]{0:T(1024)}, u32[]{:S(2)}) copy-start(f32[577]{0:T(1024)} %add_rsqrt_fusion.2) | copy-start | bytes 6928
  579.5 55.8 %copy-start.53 = (f32[1,1024]{1,0:T(1,128)S(1)}, f32[1,1024]{1,0:T(1,128)}, u32[]{:S(2)}) copy-start(f32[1,1024]{1,0:T(1,128)} %get-tuple-element.115) | copy-start | bytes 12292
  579.5 298.0 %reduce-scatter.11.cloned.1.call-start = ((), (), s32[]{:S(2)}) async-start(), calls=%async_computation.15 | async-start | bytes 1769472 | tf_op jit(solution)/shard_map/reduce_scatter | solution.py:225
  583.8 367.1 %reduce-scatter.13.cloned.1.call-start = ((), (), s32[]{:S(2)}) async-start(), calls=%async_computation.16 | async-start | bytes 589824 | tf_op jit(solution)/shard_map/reduce_scatter | solution.py:226
  635.3 4.1 copy-start.1
  635.3 4.1 copy-start.13
  639.4 4.6 copy-start.24
  645.3 384.8 %reduce-scatter.17.cloned.1.call-start = ((), (), s32[]{:S(2)}) async-start(), calls=%async_computation.18 | async-start | bytes 2359296 | tf_op jit(solution)/shard_map/reduce_scatter | solution.py:227
  649.8 458.6 %reduce-scatter.21.cloned.1.call-start = ((), (), s32[]{:S(2)}) async-start(), calls=%async_computation.20 | async-start | bytes 2359296 | tf_op jit(solution)/shard_map/reduce_scatter | solution.py:228
  654.3 4.9 copy-start.70
  654.3 530.8 %reduce-scatter.9.cloned.1.call-start = ((), (), s32[]{:S(2)}) async-start(), calls=%async_computation.14 | async-start | bytes 1769472 | tf_op jit(solution)/shard_map/reduce_scatter | solution.py:225
  662.5 7.6 copy-start.83
  670.0 7.1 copy-start.26
  676.3 4.1 copy-start.48
  676.3 4.1 copy-start.51
  676.3 4.1 copy-start.74
  684.4 4.0 copy-start.34
  684.4 500.7 %all-reduce.24.cloned.1.call-start = ((), (), s32[]{:S(2)}) async-start(), calls=%async_computation.26 | async-start | bytes 9568256 | tf_op jit(solution)/shard_map/psum | solution.py:68
  690.8 581.7 %all-reduce.26.cloned.1.call-start = ((), (), s32[]{:S(2)}) async-start(), calls=%async_computation.27 | async-start | bytes 3145728 | tf_op jit(solution)/shard_map/psum | solution.py:230
  1272.5 5.3 copy-start.43
  1272.5 5.3 copy-start.44
  (61 other events, 149.3 us)
Sparse Core Ops, SparseCore 0:
  93.5 67.2 all-reduce.11
  194.7 65.6 all-reduce.13
  284.8 63.4 all-reduce.15
  385.3 64.8 all-reduce.17
  489.7 66.1 all-reduce.19
  568.3 66.8 all-reduce.21
  691.0 75.1 all-reduce.23
  1185.2 59.1 all-reduce.25
Sparse Core Ops, SparseCore 1:
  97.1 46.6 all-gather.12
  146.6 44.1 all-gather.14
  288.3 42.8 all-gather.16
  334.2 44.1 all-gather.18
  573.1 70.1 reduce-scatter.14
  648.0 74.6 reduce-scatter.18
  726.7 74.3 reduce-scatter.22
  805.0 72.4 reduce-scatter.10
  881.5 69.4 reduce-scatter.12
  955.7 74.3 reduce-scatter.16
  1034.1 74.2 reduce-scatter.20
  1112.5 72.5 reduce-scatter.8
where the time goes:
time: 1290 us
  waiting for transfers between devices  848 us (66%)
  blocking collectives  216 us (17%)
  matrix products  117 us (9%)
  other arithmetic  47.2 us (4%)
  local copies, waits for them, and re-layouts  39.8 us (3%)
  between operations  17.3 us (1%)
    psum x3, waiting for transfers between devices, input_total(): return lax.psum(contrib, 'tp')  182 us
    reduce_scatter x2, waiting for transfers between devices, body(): lax.psum_scatter(d_down, 'fsdp', scatter_dimension=1, tiled=True)  157 us
    reduce_scatter x2, waiting for transfers between devices, body(): lax.psum_scatter(d_qkv, 'fsdp', scatter_dimension=0, tiled=True)  153 us
    psum x4, waiting for transfers between devices, branch_total(): return lax.psum(contrib, 'tp')  126 us
    reduce_scatter x2, waiting for transfers between devices, body(): lax.psum_scatter(d_up, 'fsdp', scatter_dimension=0, tiled=True)  109 us
    all_gather x2, blocking collectives, body(): lax.all_gather(qkv_weight[layer_idx], 'fsdp', axis=0, tiled=True)  78.1 us
    reduce_scatter x2, waiting for transfers between devices, body(): lax.psum_scatter(d_out, 'fsdp', scatter_dimension=1, tiled=True)  73.4 us
    psum x1, blocking collectives, body(): lax.psum((small_stack[0], small_stack[1], small_stack[2], small_stack[3],...  73.4 us
  transfers between devices with their start and end apart: 20, of which 14 were waited for; matrix products, arithmetic and copies ran while one was open for 8% of the time, Pallas kernels for 0%

commit v1 on v0

--- a/solution.py
+++ b/solution.py
@@ -5,6 +5,7 @@
 
 HEAD_DIM = 64
 EPSILON = 1e-05
+number_the_edges = lambda vals: jnp.sum(lax.all_gather(vals, "tp"), axis=0)
 
 
 def norm_forward(values_in, norm_gain, norm_shift):
@@ -69,7 +70,7 @@
 
 
 def input_total(contrib):
-    return lax.psum(contrib, "tp")
+    return number_the_edges(contrib)
 
 
 def body(

time: 1290 us -> 1530 us (1.19)
  waiting for transfers between devices: 848 us -> 1040 us
  other arithmetic: 47.2 us -> 93.2 us
    all_gather x0 -> x4, waiting for transfers between devices: none -> 282 us  [number_the_edges = lambda vals: jnp.sum(lax.all_gather(vals, 'tp'), axis=0)]
    psum x3 -> x0, waiting for transfers between devices: 182 us -> none  [input_total(): return lax.psum(contrib, 'tp')]
    reduce_scatter x2, waiting for transfers between devices: 73.4 us -> 147 us  [body(): lax.psum_scatter(d_out, 'fsdp', scatter_dimension=1, tiled=True)]
    reduce_scatter x2, waiting for transfers between devices: 157 us -> 99.9 us  [body(): lax.psum_scatter(d_down, 'fsdp', scatter_dimension=1, tiled=True)]
    psum x4, waiting for transfers between devices: 126 us -> 179 us  [branch_total(): return lax.psum(contrib, 'tp')]
    psum x1, waiting for transfers between devices: 0.01 us -> 52.1 us  [body(): lax.psum((shares[0], shares[1], shares[2], shares[3]), 'rep')]
    reduce_sum x0 -> x4, other arithmetic: none -> 44.9 us  [the longest x2 22.5 us: body(): d_shift_two = jnp.sum(d_norm_two, 0)]
    reduce_scatter x2, waiting for transfers between devices: 109 us -> 78.6 us  [body(): lax.psum_scatter(d_up, 'fsdp', scatter_dimension=0, tiled=True)]
  transfers between devices with their start and end apart: 20 -> 21, of which waited for: 14 -> 17; matrix products, arithmetic and copies ran while one was open for 8% -> 8% of each run, Pallas kernels for 0% -> 0%
where the time goes in v1:
time: 1530 us; the launch traced here: 1520 us
  waiting for transfers between devices  1040 us (68%)
  blocking collectives  216 us (14%)
  matrix products  110 us (7%)
  other arithmetic  93.2 us (6%)
  local copies, waits for them, and re-layouts  46.3 us (3%)
  between operations  17.1 us (1%)
    all_gather x4, waiting for transfers between devices, number_the_edges = lambda vals: jnp.sum(lax.all_gather(vals, 'tp'), axis=0)  282 us
    psum x4, waiting for transfers between devices, branch_total(): return lax.psum(contrib, 'tp')  179 us
    reduce_scatter x2, waiting for transfers between devices, body(): lax.psum_scatter(d_qkv, 'fsdp', scatter_dimension=0, tiled=True)  154 us
    reduce_scatter x2, waiting for transfers between devices, body(): lax.psum_scatter(d_out, 'fsdp', scatter_dimension=1, tiled=True)  147 us
    reduce_scatter x2, waiting for transfers between devices, body(): lax.psum_scatter(d_down, 'fsdp', scatter_dimension=1, tiled=True)  99.9 us
    reduce_scatter x2, waiting for transfers between devices, body(): lax.psum_scatter(d_up, 'fsdp', scatter_dimension=0, tiled=True)  78.6 us
    all_gather x2, blocking collectives, body(): lax.all_gather(qkv_weight[layer_idx], 'fsdp', axis=0, tiled=True)  76.3 us
    psum x1, blocking collectives, body(): lax.psum((small_stack[0], small_stack[1], small_stack[2], small_stack[3],...  75.3 us
  transfers between devices with their start and end apart: 21, of which 17 were waited for; matrix products, arithmetic and copies ran while one was open for 8% of the time, Pallas kernels for 0%

profile of v1, /device:TPU:0, one launch (start us, length us, event | category | flops | bytes accessed | tf_op | source)
XLA Modules:
  0.0 1523.2 jit_solution(12934431218995740970)
XLA Ops:
  12.7 38.1 %all-gather = bf16[1,1024,3,128]{3,1,2,0:T(8,128)(2,1)S(1)} all-gather(bf16[1,128,3,128]{3,1,2,0:T(8,128)(2,1)S(1)} %get-tuple-element.126), channel_id=2, replica_groups=mesh['rep'=2,'fsdp'=8,'tp'=8] {'fsdp'}, dimensions={1}, use_global_device_ids=true | all-gather | bytes 884736 | tf_op jit(solution)/shard_map/all_gather | solution.py:103
  57.9 31.6 %all-gather.1 = bf16[1,128,1024]{2,1,0:T(8,128)(2,1)S(1)} all-gather(bf16[1,128,128]{2,1,0:T(8,128)(2,1)S(1)} %get-tuple-element.128), channel_id=3, replica_groups=mesh['rep'=2,'fsdp'=8,'tp'=8] {'fsdp'}, dimensions={2}, use_global_device_ids=true | all-gather | bytes 294912 | tf_op jit(solution)/shard_map/all_gather | solution.py:104
  96.3 63.3 %all-reduce.8.cloned.1.call-done = f32[577,1024]{1,0:T(8,128)} async-done(((f32[577,1024]{1,0:T(8,128)}), f32[577,1024]{1,0:T(8,128)}) %all-reduce.8.cloned.1.call-update) | async-done | bytes 2363408 | tf_op jit(solution)/shard_map/psum | solution.py:69
  165.8 23.8 %all-gather.27.cloned.1.call-done = bf16[1,512,1024]{2,1,0:T(8,128)(2,1)} async-done(((bf16[1,512,128]{2,1,0:T(8,128)(2,1)}), bf16[1,512,1024]{2,1,0:T(8,128)(2,1)}) %all-gather.27.cloned.1.call-update) | async-done | bytes 1048592 | tf_op jit(solution)/shard_map/all_gather | solution.py:106
  189.6 3.8 fusion.77
  194.7 32.9 %all-gather.5 = bf16[1,128,1024]{2,1,0:T(8,128)(2,1)} all-gather(bf16[1,128,128]{2,1,0:T(8,128)(2,1)S(1)} %get-tuple-element.127), channel_id=7, replica_groups=mesh['rep'=2,'fsdp'=8,'tp'=8] {'fsdp'}, dimensions={2}, use_global_device_ids=true | all-gather | bytes 294912 | tf_op jit(solution)/shard_map/all_gather | solution.py:104
  228.3 38.2 %all-gather.4 = bf16[1,1024,3,128]{3,1,2,0:T(8,128)(2,1)S(1)} all-gather(bf16[1,128,3,128]{3,1,2,0:T(8,128)(2,1)} %get-tuple-element.125), channel_id=6, replica_groups=mesh['rep'=2,'fsdp'=8,'tp'=8] {'fsdp'}, dimensions={1}, use_global_device_ids=true | all-gather | bytes 884736 | tf_op jit(solution)/shard_map/all_gather | solution.py:103
  287.8 62.1 %all-reduce.12.cloned.1.call-done = f32[577,1024]{1,0:T(8,128)} async-done(((f32[577,1024]{1,0:T(8,128)}), f32[577,1024]{1,0:T(8,128)}) %all-reduce.12.cloned.1.call-update) | async-done | bytes 2363408 | tf_op jit(solution)/shard_map/psum | solution.py:69
  354.6 4.0 convolution_add_fusion
  358.6 20.9 %all-gather.31.cloned.1.call-done = bf16[1,512,1024]{2,1,0:T(8,128)(2,1)} async-done(((bf16[1,512,128]{2,1,0:T(8,128)(2,1)}), bf16[1,512,1024]{2,1,0:T(8,128)(2,1)}) %all-gather.31.cloned.1.call-update) | async-done | bytes 1048592 | tf_op jit(solution)/shard_map/all_gather | solution.py:106
  379.5 3.7 fusion.175
  386.4 3.9 fusion.72
  390.5 89.0 %all-gather.33.cloned.1.call-done = f32[8,577,1024]{2,1,0:T(8,128)} async-done(((f32[1,577,1024]{2,1,0:T(8,128)}), f32[8,577,1024]{2,1,0:T(8,128)}) %all-gather.33.cloned.1.call-update) | async-done | bytes 18907152 | tf_op jit(solution)/shard_map/all_gather | solution.py:8
  479.4 11.2 fusion.143
  490.7 3.9 multiply_reduce_fusion.4
  495.2 54.1 %all-reduce.14.cloned.1.call-done = f32[577,1024]{1,0:T(8,128)} async-done(((f32[577,1024]{1,0:T(8,128)}), f32[577,1024]{1,0:T(8,128)}) %all-reduce.14.cloned.1.call-update) | async-done | bytes 2363408 | tf_op jit(solution)/shard_map/psum | solution.py:69
  549.3 5.8 fusion.148
  559.3 3.4 fusion.116
  562.7 7.3 fusion.158
  570.0 6.8 fusion.68
  576.8 3.8 fusion.159
  589.3 94.2 %all-gather.35.cloned.1.call-done = f32[8,577,1024]{2,1,0:T(8,128)} async-done(((f32[1,577,1024]{2,1,0:T(8,128)}), f32[8,577,1024]{2,1,0:T(8,128)}) %all-gather.35.cloned.1.call-update) | async-done | bytes 18907152 | tf_op jit(solution)/shard_map/all_gather | solution.py:8
  683.4 11.2 fusion.145
  694.7 4.1 multiply_reduce_fusion.6
  707.0 4.4 fusion.99
  711.4 4.0 fusion.56
  715.6 3.4 fusion.93
  719.1 4.6 fusion.113
  724.3 3.7 fusion.96
  728.1 4.4 fusion.90
  732.6 70.0 %all-gather.37.cloned.1.call-done = f32[8,577,1024]{2,1,0:T(8,128)} async-done(((f32[1,577,1024]{2,1,0:T(8,128)}), f32[8,577,1024]{2,1,0:T(8,128)}) %all-gather.37.cloned.1.call-update) | async-done | bytes 18907152 | tf_op jit(solution)/shard_map/all_gather | solution.py:8
  802.6 11.3 fusion.142
  825.6 5.7 fusion.156
  833.0 5.0 fusion.65
  840.7 3.8 fusion.112
  844.6 21.9 %reduce-scatter.23.cloned.1.call-done = f32[512,128]{1,0:T(8,128)} async-done(((f32[512,1024]{1,0:T(8,128)}), f32[512,128]{1,0:T(8,128)}) %reduce-scatter.23.cloned.1.call-update) | async-done | bytes 262160 | tf_op jit(solution)/shard_map/reduce_scatter | solution.py:229
  866.5 73.3 %reduce-scatter.15.cloned.1.call-done = f32[128,128]{1,0:T(8,128)} async-done(((f32[128,1024]{1,0:T(8,128)}), f32[128,128]{1,0:T(8,128)}) %reduce-scatter.15.cloned.1.call-update) | async-done | bytes 65552 | tf_op jit(solution)/shard_map/reduce_scatter | solution.py:227
  939.8 76.7 %reduce-scatter.11.cloned.1.call-done = f32[128,3,128]{2,0,1:T(8,128)} async-done(((f32[1024,3,128]{2,0,1:T(8,128)}), f32[128,3,128]{2,0,1:T(8,128)}) %reduce-scatter.11.cloned.1.call-update) | async-done | bytes 196624 | tf_op jit(solution)/shard_map/reduce_scatter | solution.py:226
  1016.6 78.5 %reduce-scatter.17.cloned.1.call-done = f32[128,512]{1,0:T(8,128)} async-done(((f32[1024,512]{1,0:T(8,128)}), f32[128,512]{1,0:T(8,128)}) %reduce-scatter.17.cloned.1.call-update) | async-done | bytes 262160 | tf_op jit(solution)/shard_map/reduce_scatter | solution.py:228
  1095.1 78.0 %reduce-scatter.21.cloned.1.call-done = f32[512,128]{1,0:T(8,128)} async-done(((f32[512,1024]{1,0:T(8,128)}), f32[512,128]{1,0:T(8,128)}) %reduce-scatter.21.cloned.1.call-update) | async-done | bytes 262160 | tf_op jit(solution)/shard_map/reduce_scatter | solution.py:229
  1173.1 73.3 %reduce-scatter.13.cloned.1.call-done = f32[128,128]{1,0:T(8,128)} async-done(((f32[128,1024]{1,0:T(8,128)}), f32[128,128]{1,0:T(8,128)}) %reduce-scatter.13.cloned.1.call-update) | async-done | bytes 65552 | tf_op jit(solution)/shard_map/reduce_scatter | solution.py:227
  1246.4 77.0 %reduce-scatter.9.cloned.1.call-done = f32[128,3,128]{2,0,1:T(8,128)} async-done(((f32[1024,3,128]{2,0,1:T(8,128)}), f32[128,3,128]{2,0,1:T(8,128)}) %reduce-scatter.9.cloned.1.call-update) | async-done | bytes 196624 | tf_op jit(solution)/shard_map/reduce_scatter | solution.py:226
  1327.9 3.8 copy.102
  1332.1 52.1 %all-reduce.16.cloned.1.call-done = (f32[1,128,3,128]{3,1,2,0:T(8,128)}, f32[1,128,3,128]{3,1,2,0:T(8,128)}, f32[1,128,128]{2,1,0:T(8,128)}, f32[1,128,128]{2,1,...) async-done(((f32[1,128,3,128]{3,1,2,0:T(8,128)}, f32[1,128,3,128]{3,1,2,0:T(8,128)}, ...) | async-done | bytes 1572880 | tf_op jit(solution)/shard_map/psum | solution.py:231
  1391.3 28.4 %all-gather.39.cloned.1.call-done = f32[8,577,1024]{2,1,0:T(8,128)} async-done(((f32[1,577,1024]{2,1,0:T(8,128)}), f32[8,577,1024]{2,1,0:T(8,128)}) %all-gather.39.cloned.1.call-update) | async-done | bytes 18907152 | tf_op jit(solution)/shard_map/all_gather | solution.py:8
  1419.7 11.2 fusion.144
  1436.3 3.8 copy.103
  1440.2 75.3 %all-reduce = (f32[2,1024]{1,0:T(2,128)}, f32[2,1024]{1,0:T(2,128)}, f32[2,2,128]{2,1,0:T(2,128)}, f32[2,1024]{1,0:T(2,128)}, f32[2,1024]{1,0:T(2,128)}, /*index...) all-reduce(f32[2,1024]{1,0:T(2,128)S(1)} %pad_maximum_fusion.10, ...), channel_id=1, replica_groups=mesh['rep'=2,'fsdp'=8,'tp'=8] {'rep','fsdp'}, use_global_device_ids=true, to_apply=%region_32.0 | all-reduce | flops 13824 | bytes 110592 | tf_op jit(solution)/shard_map/psum | solution.py:242
  (328 shorter events, 111.1 us)
Async XLA Ops:
  8.0 43.5 %copy-start.10 = (bf16[1,577,1024]{2,1,0:T(8,128)(2,1)S(1)}, bf16[1,577,1024]{2,1,0:T(8,128)(2,1)}, u32[]{:S(2)}) copy-start(bf16[1,577,1024]{2,1,0:T(8,128)(2,1)} %param.14) | copy-start | bytes 3545092
  8.0 42.8 %copy-start.62 = (f32[2,1024]{1,0:T(2,128)S(1)}, f32[2,1024]{1,0:T(2,128)}, u32[]{:S(2)}) copy-start(f32[2,1024]{1,0:T(2,128)} %param.17) | copy-start | bytes 24580
  8.1 151.5 %all-reduce.8.cloned.1.call-start = ((), (), s32[]{:S(2)}) async-start(), calls=%async_computation.8 | async-start | bytes 4784128 | tf_op jit(solution)/shard_map/psum | solution.py:69
  11.5 41.1 %copy-start.44 = (f32[577]{0:T(1024)}, f32[577]{0:T(1024)S(1)}, u32[]{:S(2)}) copy-start(f32[577]{0:T(1024)S(1)} %add_rsqrt_fusion.3) | copy-start | bytes 6928
  12.1 40.5 %copy-start.48 = (f32[1,1024]{1,0:T(1,128)}, f32[1,1024]{1,0:T(1,128)S(1)}, u32[]{:S(2)}) copy-start(f32[1,1024]{1,0:T(1,128)S(1)} %get-tuple-element.136) | copy-start | bytes 12292
  55.1 35.1 %copy-start.2 = (f32[2,577,577]{1,2,0:T(8,128)}, f32[2,577,577]{1,2,0:T(8,128)S(1)}, u32[]{:S(2)}) copy-start(f32[2,577,577]{1,2,0:T(8,128)S(1)} %get-tuple-element.144) | copy-start | bytes 7990300
  57.2 35.1 %copy-start.67 = (f32[2,64]{1,0:T(2,128)}, f32[2,64]{1,0:T(2,128)S(1)}, u32[]{:S(2)}) copy-start(f32[2,64]{1,0:T(2,128)S(1)} %add.296) | copy-start | bytes 1540
  92.3 70.2 %all-gather.25.cloned.1.call-start = ((), (), s32[]{:S(2)}) async-start(), calls=%async_computation.20 | async-start | bytes 1179648 | tf_op jit(solution)/shard_map/all_gather | solution.py:105
  93.1 96.5 %all-gather.27.cloned.1.call-start = ((), (), s32[]{:S(2)}) async-start(), calls=%async_computation.21 | async-start | bytes 1179648 | tf_op jit(solution)/shard_map/all_gather | solution.py:106
  93.9 172.6 %all-reduce.10.cloned.1.call-start = ((), (), s32[]{:S(2)}) async-start(), calls=%async_computation.9 | async-start | bytes 4784128 | tf_op jit(solution)/shard_map/psum | solution.py:69
  95.1 67.3 %copy-start.51 = (f32[1,1024]{1,0:T(1,128)}, f32[1,1024]{1,0:T(1,128)S(1)}, u32[]{:S(2)}) copy-start(f32[1,1024]{1,0:T(1,128)S(1)} %get-tuple-element.132) | copy-start | bytes 12292
  96.3 66.2 %copy-start.75 = (f32[1,1024]{1,0:T(1,128)}, f32[1,1024]{1,0:T(1,128)S(1)}, u32[]{:S(2)}) copy-start(f32[1,1024]{1,0:T(1,128)S(1)} %get-tuple-element.134) | copy-start | bytes 12292
  165.8 27.7 %copy-start.86 = (f32[128]{0:T(128)S(1)}, f32[128]{0:T(128)}, u32[]{:S(2)}) copy-start(f32[128]{0:T(128)} %get-tuple-element.79) | copy-start | bytes 1540
  165.8 28.4 %copy-start.85 = (f32[128]{0:T(128)S(1)}, f32[128]{0:T(128)}, u32[]{:S(2)}) copy-start(f32[128]{0:T(128)} %get-tuple-element.76) | copy-start | bytes 1540
  193.4 34.3 %copy-start.66 = (f32[2,1024]{1,0:T(2,128)S(1)}, f32[2,1024]{1,0:T(2,128)}, u32[]{:S(2)}) copy-start(f32[2,1024]{1,0:T(2,128)} %param.27) | copy-start | bytes 24580
  193.4 156.6 %all-reduce.12.cloned.1.call-start = ((), (), s32[]{:S(2)}) async-start(), calls=%async_computation.10 | async-start | bytes 4784128 | tf_op jit(solution)/shard_map/psum | solution.py:69
  270.3 5.1 copy-start.84
  284.5 65.4 %copy-start.60 = (f32[1,1024]{1,0:T(1,128)S(1)}, f32[1,1024]{1,0:T(1,128)}, u32[]{:S(2)}) copy-start(f32[1,1024]{1,0:T(1,128)} %get-tuple-element.140) | copy-start | bytes 12292
  286.4 68.1 %all-gather.29.cloned.1.call-start = ((), (), s32[]{:S(2)}) async-start(), calls=%async_computation.22 | async-start | bytes 1179648 | tf_op jit(solution)/shard_map/all_gather | solution.py:105
  287.0 92.5 %all-gather.31.cloned.1.call-start = ((), (), s32[]{:S(2)}) async-start(), calls=%async_computation.23 | async-start | bytes 1179648 | tf_op jit(solution)/shard_map/all_gather | solution.py:106
  287.8 191.7 %all-gather.33.cloned.1.call-start = ((), (), s32[]{:S(2)}) async-start(), calls=%async_computation.24 | async-start | bytes 21528576 | tf_op jit(solution)/shard_map/all_gather | solution.py:8
  379.5 4.6 copy-start.31
  386.3 162.9 %all-reduce.14.cloned.1.call-start = ((), (), s32[]{:S(2)}) async-start(), calls=%async_computation.11 | async-start | bytes 4784128 | tf_op jit(solution)/shard_map/psum | solution.py:69
  390.3 293.2 %all-gather.35.cloned.1.call-start = ((), (), s32[]{:S(2)}) async-start(), calls=%async_computation.25 | async-start | bytes 21528576 | tf_op jit(solution)/shard_map/all_gather | solution.py:8
  549.3 7.2 copy-start.22
  589.0 213.6 %all-gather.37.cloned.1.call-start = ((), (), s32[]{:S(2)}) async-start(), calls=%async_computation.26 | async-start | bytes 21528576 | tf_op jit(solution)/shard_map/all_gather | solution.py:8
  706.9 137.7 %reduce-scatter.19.cloned.1.call-start = ((), (), s32[]{:S(2)}) async-start(), calls=%async_computation.17 | async-start | bytes 2359296 | tf_op jit(solution)/shard_map/reduce_scatter | solution.py:228
  711.4 4.2 copy-start.26
  711.4 155.1 %reduce-scatter.23.cloned.1.call-start = ((), (), s32[]{:S(2)}) async-start(), calls=%async_computation.19 | async-start | bytes 2359296 | tf_op jit(solution)/shard_map/reduce_scatter | solution.py:229
  715.5 224.3 %reduce-scatter.15.cloned.1.call-start = ((), (), s32[]{:S(2)}) async-start(), calls=%async_computation.15 | async-start | bytes 589824 | tf_op jit(solution)/shard_map/reduce_scatter | solution.py:227
  719.0 5.3 copy-start.47
  719.0 5.3 copy-start.52
  719.0 5.3 copy-start.76
  719.0 297.6 %reduce-scatter.11.cloned.1.call-start = ((), (), s32[]{:S(2)}) async-start(), calls=%async_computation.13 | async-start | bytes 1769472 | tf_op jit(solution)/shard_map/reduce_scatter | solution.py:226
  723.8 371.4 %reduce-scatter.17.cloned.1.call-start = ((), (), s32[]{:S(2)}) async-start(), calls=%async_computation.16 | async-start | bytes 2359296 | tf_op jit(solution)/shard_map/reduce_scatter | solution.py:228
  728.1 445.0 %reduce-scatter.21.cloned.1.call-start = ((), (), s32[]{:S(2)}) async-start(), calls=%async_computation.18 | async-start | bytes 2359296 | tf_op jit(solution)/shard_map/reduce_scatter | solution.py:229
  732.6 513.8 %reduce-scatter.13.cloned.1.call-start = ((), (), s32[]{:S(2)}) async-start(), calls=%async_computation.14 | async-start | bytes 589824 | tf_op jit(solution)/shard_map/reduce_scatter | solution.py:227
  825.5 7.5 copy-start.28
  825.5 7.5 copy-start.82
  825.5 497.8 %reduce-scatter.9.cloned.1.call-start = ((), (), s32[]{:S(2)}) async-start(), calls=%async_computation.12 | async-start | bytes 1769472 | tf_op jit(solution)/shard_map/reduce_scatter | solution.py:226
  844.5 479.1 %copy-start.18 = (bf16[1,1024,3,128]{3,1,2,0:T(8,128)(2,1)S(1)}, bf16[1,1024,3,128]{3,1,2,0:T(8,128)(2,1)}, u32[]{:S(2)}) copy-start(bf16[1,1024,3,128]{3,1,2,0:T(8,128)(2,1)} %copy-done.17) | copy-start | bytes 2359300
  844.5 479.1 %copy-start.37 = (bf16[577,1,128]{2,0,1:T(8,128)(2,1)S(1)}, bf16[577,1,128]{2,0,1:T(8,128)(2,1)}, u32[]{:S(2)}) copy-start(bf16[577,1,128]{2,0,1:T(8,128)(2,1)} %copy.100) | copy-start | bytes 443140
  844.5 539.7 %all-reduce.16.cloned.1.call-start = ((), (), s32[]{:S(2)}) async-start(), calls=%async_computation.28 | async-start | bytes 3145728 | tf_op jit(solution)/shard_map/psum | solution.py:231
  1323.4 96.3 %all-gather.39.cloned.1.call-start = ((), (), s32[]{:S(2)}) async-start(), calls=%async_computation.27 | async-start | bytes 21528576 | tf_op jit(solution)/shard_map/all_gather | solution.py:8
  1327.5 4.2 copy-start.79
  1327.5 4.2 copy-start.80
  1327.9 4.2 copy-start.58
  1391.3 39.6 %copy-start.11 = (bf16[1,577,1024]{2,1,0:T(8,128)(2,1)S(1)}, bf16[1,577,1024]{2,1,0:T(8,128)(2,1)}, u32[]{:S(2)}) copy-start(bf16[1,577,1024]{2,1,0:T(8,128)(2,1)} %param.14) | copy-start | bytes 3545092
  (62 other events, 155.7 us)
Sparse Core Ops, SparseCore 0:
  92.4 67.1 all-reduce.7
  193.5 65.6 all-reduce.9
  286.6 63.3 all-reduce.11
  386.4 92.9 all-gather.32
  481.8 67.3 all-reduce.13
  589.1 94.2 all-gather.34
  707.0 95.5 all-gather.36
  1326.0 93.6 all-gather.38
Sparse Core Ops, SparseCore 1:
  95.9 46.6 all-gather.24
  145.5 44.1 all-gather.26
  290.1 42.8 all-gather.28
  335.4 44.1 all-gather.30
  712.0 76.5 reduce-scatter.18
  792.2 74.2 reduce-scatter.22
  870.5 69.3 reduce-scatter.14
  943.8 72.7 reduce-scatter.10
  1020.7 74.3 reduce-scatter.16
  1098.9 74.2 reduce-scatter.20
  1177.1 69.2 reduce-scatter.12
  1250.5 72.7 reduce-scatter.8
  1326.2 58.0 all-reduce.15
